TPU v7x, 32 devices: a whole 2x2x4 slice. The times are simulated.
32 devices in a mesh: groups: 2 (over y), res: 4 (over z), blk: 2 (over x), ch: 2 (over core).
Axes of the slice: x: 2, y: 2, z: 4, core: 2. Of those that a mesh axis runs over, the one named last changes fastest.
Arguments:
- single: bfloat16 [16384, 384], P(('groups', 'res')), parts along dimension 0, may hold values from -6 to 6
- frames: float32 [12, 16384], P(None, ('groups', 'res')), parts along dimension 1
- teacher: float32 [12, 16384], P(None, ('groups', 'res')), parts along dimension 1
- res_mask: int32 [16384], P(('groups', 'res')), parts along dimension 0, may hold values 0 or 1
- chain_ids: int32 [16384], P(('groups', 'res')), parts along dimension 0, may hold values from 0 to 31, never falling along the last dimension, each value on 1 to 512 neighbouring positions
- block_pairs: int32 [16, 12, 2], P('groups'), parts along dimension 0, may hold values from 0 to 63, as said below
- w_left: bfloat16 [384, 128], replicated, may hold values from -0.3125 to 0.3125
- w_right: bfloat16 [384, 128], replicated, may hold values from -0.3125 to 0.3125
- w_value: bfloat16 [384, 128], replicated, may hold values from -0.3125 to 0.3125
- w_pair: bfloat16 [128, 128], P(None, 'ch'), may hold values from -0.5 to 0.5
- pair_bias: float32 [128], P('ch'), may hold values from -3 to 3
- gate_vec: float32 [128], P('ch'), may hold values from -1 to 1
- w_out: bfloat16 [128, 384], replicated, may hold values from -0.5 to 0.5
Outputs:
- updated: bfloat16 [16384, 384], P(('groups', 'res')), parts along dimension 0
- pair_fape: float32 [192], P(('groups', 'res', 'blk')), parts along dimension 0
There are 2 independent parts, one for each index of `groups`. A program takes and returns all parts, laid end to end along the dimension named above; an argument that names none is the same for every part. Nothing has to cross between parts.
Inputs may be any that keep to these rules, and one draw needn't show every extreme that they name: block_pairs[o,p,0] lies in blocks (o // 2) * 16 to (o // 2 + 1) * 16 - 1. Among the 12 pairs of one owner at most 4 have their second block in one run of blocks k * 16 to (k+1) * 16 - 1, and in every draw each owner has exactly 4 in one such run.
All inputs are finite; a program needn't handle non-finite values. No bound on the sum of `res_mask` on one device may be relied on, other than what follows from the above.
Results may differ from a plain program's by a relative error of at most 0.0059.
Values may be sent and summed in bfloat16 or wider, within the bound.
A program may use at most 64 MiB of HBM per device.

v0:
```python
import jax
import jax.numpy as jnp
from jax import lax
from jax.sharding import PartitionSpec as P

BLOCK = 128


def tile_logit(near_left, far_right, w_pair, pair_bias, gate_vec):
    outer_prod = (
        near_left.astype(jnp.float32)[:, :, None] * far_right.astype(jnp.float32).T[None, :, :]
    ).astype(jnp.bfloat16)
    pair_act = jnp.einsum("kc,akb->acb", w_pair, outer_prod, preferred_element_type=jnp.float32)
    pair_act = pair_act + pair_bias[None, :, None]
    return jnp.einsum(
        "c,acb->ab", gate_vec, jnp.maximum(pair_act, 0.0), precision=lax.Precision.HIGHEST
    )


def local_coords(geo_near, geo_far, offset):
    coords = []
    for axis_k in range(3):
        summed = jnp.zeros(
            geo_near.shape[:-2] + (geo_near.shape[-1], geo_far.shape[-1]), jnp.float32
        )
        for axis_m in range(3):
            gap_vec = (
                geo_far[..., offset + 9 + axis_m, None, :]
                - geo_near[..., offset + 9 + axis_m, :, None]
            )
            summed = summed + geo_near[..., offset + 3 * axis_m + axis_k, :, None] * gap_vec
        coords.append(summed)
    return coords


def finish(logit, value_near, value_far, geo_near, geo_far):
    live = geo_near[..., 24, :, None] * geo_far[..., 24, None, :]
    live = live * (geo_near[..., 25, :, None] != geo_far[..., 25, None, :]).astype(jnp.float32)
    weight = jax.nn.sigmoid(logit) * live
    weight_low = weight.astype(jnp.bfloat16)
    scale = BLOCK ** (-0.5)
    to_second = jnp.einsum(
        "pab,pac->pbc", weight_low, value_near, preferred_element_type=jnp.float32
    )
    to_second = (to_second * scale).astype(jnp.bfloat16)
    to_first = jnp.einsum("pab,pbc->pac", weight_low, value_far, preferred_element_type=jnp.float32)
    to_first = (to_first * scale).astype(jnp.bfloat16)
    pred_coords = local_coords(geo_near, geo_far, 0)
    true_coords = local_coords(geo_near, geo_far, 12)
    dist_sq = jnp.zeros_like(weight)
    for axis_k in range(3):
        dist_sq = dist_sq + (pred_coords[axis_k] - true_coords[axis_k]) ** 2
    clipped = jnp.minimum(jnp.sqrt(dist_sq + 0.0001), 10.0)
    fape_value = jnp.sum(weight * clipped, axis=(1, 2)) / (BLOCK * BLOCK)
    return (fape_value, to_first, to_second)


def shards(
    single,
    frames,
    teacher,
    res_mask,
    chain_ids,
    block_pairs,
    w_left,
    w_right,
    w_value,
    w_pair,
    pair_bias,
    gate_vec,
    w_out,
):
    res_count = lax.axis_size("res")
    blk_count = lax.axis_size("blk")
    res_rank = lax.axis_index("res")
    blk_rank = lax.axis_index("blk")
    row_count = single.shape[0]
    feat_width = single.shape[1]
    blocks_here = row_count // BLOCK
    pair_dev = block_pairs.shape[1]
    capacity = 1 + (pair_dev + res_count - 2) // res_count
    msg_width = w_value.shape[1]
    owner_table = block_pairs.reshape(res_count, blk_count, pair_dev, 2)
    column_pairs = lax.dynamic_index_in_dim(owner_table, blk_rank, 1, keepdims=False)
    own_pairs = lax.dynamic_index_in_dim(column_pairs, res_rank, 0, keepdims=False)
    wanted_ids = column_pairs[:, :, 1]
    hit_flags = (wanted_ids // blocks_here == res_rank).astype(jnp.int32)
    hit_rank = jnp.cumsum(hit_flags, axis=1) - 1
    slot_ids = jnp.arange(capacity, dtype=jnp.int32)
    picked = hit_flags[:, None, :] * (hit_rank[:, None, :] == slot_ids[None, :, None]).astype(
        jnp.int32
    )
    send_local = jnp.sum(
        picked * (wanted_ids - res_rank * blocks_here)[:, None, :], axis=2
    ).reshape(-1)
    send_valid = jnp.sum(picked, axis=2).reshape(-1)
    geometry = jnp.concatenate(
        [
            frames,
            teacher,
            res_mask[None, :].astype(jnp.float32),
            chain_ids[None, :].astype(jnp.float32),
        ],
        axis=0,
    )
    geo_blocks = geometry.reshape(26, blocks_here, BLOCK).transpose(1, 0, 2)
    geo_send = jnp.take(geo_blocks, send_local, axis=0).reshape(res_count, capacity, 26, BLOCK)
    first_local = own_pairs[:, 0] - res_rank * blocks_here
    source_shard = own_pairs[:, 1] // blocks_here
    pair_index = jnp.arange(pair_dev, dtype=jnp.int32)
    earlier = (source_shard[None, :] == source_shard[:, None]) & (
        pair_index[None, :] < pair_index[:, None]
    )
    recv_slot = source_shard * capacity + jnp.sum(earlier.astype(jnp.int32), axis=1)
    single_blocks = single.reshape(blocks_here, BLOCK, feat_width)
    row_send = jnp.take(single_blocks, send_local, axis=0).reshape(
        res_count, capacity, BLOCK, feat_width
    )
    row_recv = lax.all_to_all(row_send, "res", split_axis=0, concat_axis=0, tiled=True)
    far_rows = jnp.take(row_recv.reshape(-1, BLOCK, feat_width), recv_slot, axis=0)
    near_rows = jnp.take(single_blocks, first_local, axis=0)
    left_feats = jnp.einsum(
        "pad,dc->pac", near_rows, w_left, preferred_element_type=jnp.float32
    ).astype(jnp.bfloat16)
    value_near = jnp.einsum(
        "pad,dc->pac", near_rows, w_value, preferred_element_type=jnp.float32
    ).astype(jnp.bfloat16)
    right_feats = jnp.einsum(
        "pad,dc->pac", far_rows, w_right, preferred_element_type=jnp.float32
    ).astype(jnp.bfloat16)
    value_far = jnp.einsum(
        "pad,dc->pac", far_rows, w_value, preferred_element_type=jnp.float32
    ).astype(jnp.bfloat16)
    geo_recv = lax.all_to_all(
        geo_send.astype(jnp.bfloat16), "res", split_axis=0, concat_axis=0, tiled=True
    ).astype(geo_send.dtype)
    far_geo = jnp.take(geo_recv.reshape(-1, 26, BLOCK), recv_slot, axis=0)
    near_geo = jnp.take(geo_blocks, first_local, axis=0)

    def tile_step(state_in, tile_inputs):
        return (state_in, tile_logit(tile_inputs[0], tile_inputs[1], w_pair, pair_bias, gate_vec))

    state_out, partial_logits = lax.scan(
        tile_step, jnp.zeros((), jnp.float32), (left_feats, right_feats)
    )
    logits = lax.psum(partial_logits, "ch")
    pair_fape, to_first, to_second = finish(logits, value_near, value_far, near_geo, far_geo)
    back_hot = (
        recv_slot[:, None] == jnp.arange(res_count * capacity, dtype=jnp.int32)[None, :]
    ).astype(jnp.bfloat16)
    back_buffer = jnp.einsum(
        "ps,pbc->sbc", back_hot, to_second, preferred_element_type=jnp.float32
    ).astype(jnp.bfloat16)
    back_buffer = back_buffer.reshape(res_count, capacity, BLOCK, msg_width)
    returned = lax.all_to_all(back_buffer, "res", split_axis=0, concat_axis=0, tiled=True)
    block_index = jnp.arange(blocks_here, dtype=jnp.int32)
    send_hot = ((send_local[:, None] == block_index[None, :]) & (send_valid[:, None] > 0)).astype(
        jnp.bfloat16
    )
    delta_rows = jnp.einsum(
        "sl,sbc->lbc",
        send_hot,
        returned.reshape(-1, BLOCK, msg_width),
        preferred_element_type=jnp.float32,
    )
    near_hot = (first_local[:, None] == block_index[None, :]).astype(jnp.bfloat16)
    delta_rows = delta_rows + jnp.einsum(
        "pl,pac->lac", near_hot, to_first, preferred_element_type=jnp.float32
    )
    delta_rows = delta_rows.reshape(row_count, msg_width)
    summed_rows = lax.psum(delta_rows, "blk")
    updated = (
        single.astype(jnp.float32)
        + jnp.dot(summed_rows.astype(jnp.bfloat16), w_out, preferred_element_type=jnp.float32)
    ).astype(jnp.bfloat16)
    return (updated, pair_fape)


def solution(mesh):
    placed = (
        P(("groups", "res"), None),
        P(None, ("groups", "res")),
        P(None, ("groups", "res")),
        P(("groups", "res")),
        P(("groups", "res")),
        P("groups", None, None),
        P(),
        P(),
        P(),
        P(None, "ch"),
        P("ch"),
        P("ch"),
        P(),
    )
    return jax.shard_map(
        shards,
        mesh=mesh,
        in_specs=placed,
        out_specs=(P(("groups", "res"), None), P(("groups", "res", "blk"))),
        check_vma=False,
    )
```

profile of v0, /device:TPU:0, one launch (start us, length us, event | category | flops | bytes accessed | tf_op | source)
XLA Modules:
  0.0 224.0 jit_solution(8328334812829523707)
XLA Ops:
  12.7 6.4 %all-to-all-start = ((bf16[4,4,128,384]{3,2,1,0:T(8,128)(2,1)}), bf16[4,4,128,384]{3,2,1,0:T(8,128)(2,1)S(1)}, u32[]{:S(2)}, u32[]{:S(2)}) async-start(bf16[4,4,128,384]{3,2,1,0:T(8,128)(2,1)} %broadcast_select_fusion), calls=%async_computation | async-start | bytes 3145728 | tf_op jit(solution)/shard_map/all_to_all | solution.py:119
  29.8 2.6 %convolution_convert_fusion.4 = bf16[12,128,128]{2,1,0:T(8,128)(2,1)} fusion(bf16[12,128,384]{2,1,0:T(8,128)(2,1)} %gather_fusion.2, pred[12]{0:T(512)(128)(4,1)} %copy-done.26, bf16[384,128]{1,0:T(8,128)(2,1)} %param.25), kind=kOutput, calls=%fused_computation.52 | convolution fusion | flops 151781376 | bytes 1671180 | tf_op jit(solution)/shard_map/pad,dc->pac/dot_general | solution.py:122
  32.3 23.7 %all-to-all-done = bf16[4,4,128,384]{3,2,1,0:T(8,128)(2,1)S(1)} async-done(((bf16[4,4,128,384]{3,2,1,0:T(8,128)(2,1)}), bf16[4,4,128,384]{3,2,1,0:T(8,128)(2,1)S(1)}, u32[]{:S(2)}, u32[]{:S(2)}) %all-to-all-start) | async-done | bytes 1572896 | tf_op jit(solution)/shard_map/all_to_all | solution.py:119
  56.1 3.3 %all-to-all-start.1 = ((bf16[4,4,26,128]{3,1,2,0:T(4,128)(2,1)}), bf16[4,4,26,128]{3,1,2,0:T(4,128)(2,1)S(1)}, u32[]{:S(2)}, u32[]{:S(2)}) async-start(bf16[4,4,26,128]{3,1,2,0:T(4,128)(2,1)} %fusion.42), calls=%async_computation.1 | async-start | bytes 212992 | tf_op jit(solution)/shard_map/all_to_all | solution.py:134
  63.1 79.4 %while.11 = (s32[]{:T(128)}, f32[12,128,128]{2,1,0:T(8,128)}, bf16[12,128,128]{2,1,0:T(8,128)(2,1)}, bf16[12,128,128]{2,1,0:T(8,128)(2,1)S(1)}, bf16[128,64]{0,1...) while((s32[]{:T(128)}, f32[12,128,128]{2,1,0:T(8,128)}, bf16[12,128,128]{2,1,0:T(8,128)(2,1)}, ...), condition=%wide.region_5.7_spmd.clone, body=%wide.region_4.6_spmd.sunk.clone | while | flops 287342592 | bytes 9061461 | solution.py:143
  66.6 2.5 %fusion.99 = f32[1,128,128]{2,0,1:T(1,128)S(1)} fusion(f32[128,128,64]{1,2,0:T(8,128)S(1)} %fusion.98, f32[64]{0:T(128)S(1)} %get-tuple-element.199, f32[64]{0:T(128)S(1)} %get-tuple-element.200), kind=kOutput, calls=%fused_computation.8.clone.1.clone | convolution fusion | flops 14680064 | bytes 4260352 | tf_op jit(solution)/shard_map/while/body/eval_jaxpr/c,acb->ab/dot_general | solution.py:15
  73.2 2.5 %fusion.99 = f32[1,128,128]{2,0,1:T(1,128)S(1)} fusion(f32[128,128,64]{1,2,0:T(8,128)S(1)} %fusion.98, f32[64]{0:T(128)S(1)} %get-tuple-element.199, f32[64]{0:T(128)S(1)} %get-tuple-element.200), kind=kOutput, calls=%fused_computation.8.clone.1.clone | convolution fusion | flops 14680064 | bytes 4260352 | tf_op jit(solution)/shard_map/while/body/eval_jaxpr/c,acb->ab/dot_general | solution.py:15
  79.8 2.5 %fusion.99 = f32[1,128,128]{2,0,1:T(1,128)S(1)} fusion(f32[128,128,64]{1,2,0:T(8,128)S(1)} %fusion.98, f32[64]{0:T(128)S(1)} %get-tuple-element.199, f32[64]{0:T(128)S(1)} %get-tuple-element.200), kind=kOutput, calls=%fused_computation.8.clone.1.clone | convolution fusion | flops 14680064 | bytes 4260352 | tf_op jit(solution)/shard_map/while/body/eval_jaxpr/c,acb->ab/dot_general | solution.py:15
  86.5 2.5 %fusion.99 = f32[1,128,128]{2,0,1:T(1,128)S(1)} fusion(f32[128,128,64]{1,2,0:T(8,128)S(1)} %fusion.98, f32[64]{0:T(128)S(1)} %get-tuple-element.199, f32[64]{0:T(128)S(1)} %get-tuple-element.200), kind=kOutput, calls=%fused_computation.8.clone.1.clone | convolution fusion | flops 14680064 | bytes 4260352 | tf_op jit(solution)/shard_map/while/body/eval_jaxpr/c,acb->ab/dot_general | solution.py:15
  93.1 2.5 %fusion.99 = f32[1,128,128]{2,0,1:T(1,128)S(1)} fusion(f32[128,128,64]{1,2,0:T(8,128)S(1)} %fusion.98, f32[64]{0:T(128)S(1)} %get-tuple-element.199, f32[64]{0:T(128)S(1)} %get-tuple-element.200), kind=kOutput, calls=%fused_computation.8.clone.1.clone | convolution fusion | flops 14680064 | bytes 4260352 | tf_op jit(solution)/shard_map/while/body/eval_jaxpr/c,acb->ab/dot_general | solution.py:15
  99.7 2.5 %fusion.99 = f32[1,128,128]{2,0,1:T(1,128)S(1)} fusion(f32[128,128,64]{1,2,0:T(8,128)S(1)} %fusion.98, f32[64]{0:T(128)S(1)} %get-tuple-element.199, f32[64]{0:T(128)S(1)} %get-tuple-element.200), kind=kOutput, calls=%fused_computation.8.clone.1.clone | convolution fusion | flops 14680064 | bytes 4260352 | tf_op jit(solution)/shard_map/while/body/eval_jaxpr/c,acb->ab/dot_general | solution.py:15
  106.3 2.5 %fusion.99 = f32[1,128,128]{2,0,1:T(1,128)S(1)} fusion(f32[128,128,64]{1,2,0:T(8,128)S(1)} %fusion.98, f32[64]{0:T(128)S(1)} %get-tuple-element.199, f32[64]{0:T(128)S(1)} %get-tuple-element.200), kind=kOutput, calls=%fused_computation.8.clone.1.clone | convolution fusion | flops 14680064 | bytes 4260352 | tf_op jit(solution)/shard_map/while/body/eval_jaxpr/c,acb->ab/dot_general | solution.py:15
  112.9 2.5 %fusion.99 = f32[1,128,128]{2,0,1:T(1,128)S(1)} fusion(f32[128,128,64]{1,2,0:T(8,128)S(1)} %fusion.98, f32[64]{0:T(128)S(1)} %get-tuple-element.199, f32[64]{0:T(128)S(1)} %get-tuple-element.200), kind=kOutput, calls=%fused_computation.8.clone.1.clone | convolution fusion | flops 14680064 | bytes 4260352 | tf_op jit(solution)/shard_map/while/body/eval_jaxpr/c,acb->ab/dot_general | solution.py:15
  119.5 2.5 %fusion.99 = f32[1,128,128]{2,0,1:T(1,128)S(1)} fusion(f32[128,128,64]{1,2,0:T(8,128)S(1)} %fusion.98, f32[64]{0:T(128)S(1)} %get-tuple-element.199, f32[64]{0:T(128)S(1)} %get-tuple-element.200), kind=kOutput, calls=%fused_computation.8.clone.1.clone | convolution fusion | flops 14680064 | bytes 4260352 | tf_op jit(solution)/shard_map/while/body/eval_jaxpr/c,acb->ab/dot_general | solution.py:15
  123.6 2.5 %fusion.98 = f32[128,128,64]{1,2,0:T(8,128)S(1)} fusion(f32[128,128]{1,0:T(8,128)S(1)} %convert_bitcast_fusion.3, f32[128,128]{1,0:T(8,128)S(1)} %bitcast_convert_fusion.3, bf16[128,64]{0,1:T(8,128)(2,1)S(1)} %get-tuple-element.198), kind=kOutput, calls=%fused_computation.7.clone.1.clone | convolution fusion | flops 272629760 | bytes 4341760 | tf_op jit(solution)/shard_map/while/body/eval_jaxpr/kc,akb->acb/dot_general | solution.py:13
  126.2 2.5 %fusion.99 = f32[1,128,128]{2,0,1:T(1,128)S(1)} fusion(f32[128,128,64]{1,2,0:T(8,128)S(1)} %fusion.98, f32[64]{0:T(128)S(1)} %get-tuple-element.199, f32[64]{0:T(128)S(1)} %get-tuple-element.200), kind=kOutput, calls=%fused_computation.8.clone.1.clone | convolution fusion | flops 14680064 | bytes 4260352 | tf_op jit(solution)/shard_map/while/body/eval_jaxpr/c,acb->ab/dot_general | solution.py:15
  132.8 2.5 %fusion.99 = f32[1,128,128]{2,0,1:T(1,128)S(1)} fusion(f32[128,128,64]{1,2,0:T(8,128)S(1)} %fusion.98, f32[64]{0:T(128)S(1)} %get-tuple-element.199, f32[64]{0:T(128)S(1)} %get-tuple-element.200), kind=kOutput, calls=%fused_computation.8.clone.1.clone | convolution fusion | flops 14680064 | bytes 4260352 | tf_op jit(solution)/shard_map/while/body/eval_jaxpr/c,acb->ab/dot_general | solution.py:15
  139.4 2.5 %fusion.99 = f32[1,128,128]{2,0,1:T(1,128)S(1)} fusion(f32[128,128,64]{1,2,0:T(8,128)S(1)} %fusion.98, f32[64]{0:T(128)S(1)} %get-tuple-element.199, f32[64]{0:T(128)S(1)} %get-tuple-element.200), kind=kOutput, calls=%fused_computation.8.clone.1.clone | convolution fusion | flops 14680064 | bytes 4260352 | tf_op jit(solution)/shard_map/while/body/eval_jaxpr/c,acb->ab/dot_general | solution.py:15
  151.7 11.7 %all-reduce.3.cloned.1.call-done = f32[12,128,128]{2,1,0:T(8,128)} async-done(((f32[12,128,128]{2,1,0:T(8,128)}), f32[12,128,128]{2,1,0:T(8,128)}) %all-reduce.3.cloned.1.call-update) | async-done | bytes 786448 | tf_op jit(solution)/shard_map/psum | solution.py:146
  166.8 4.9 %all-to-all-start.2 = ((bf16[4,4,128,128]{3,1,2,0:T(4,128)(2,1)}), bf16[4,4,128,128]{3,1,2,0:T(4,128)(2,1)S(1)}, u32[]{:S(2)}, u32[]{:S(2)}) async-start(bf16[4,4,128,128]{3,1,2,0:T(4,128)(2,1)} %copy.48), calls=%async_computation.2 | async-start | bytes 1048576 | tf_op jit(solution)/shard_map/all_to_all | solution.py:155
  171.7 7.5 %fusion.38 = f32[12]{0:T(128)S(1)} fusion(f32[12,128]{1,0:T(8,128)S(1)} %bitcast.233, f32[12,128]{1,0:T(8,128)S(1)} %bitcast.234, f32[12,128]{1,0:T(8,128)S(1)} %bitcast.235, f32[12,128]{1,0:T(8,128)S(1)} %bitcast.236, f32[12,128]{1,0:T(8,128)S(1)} %bitcast.240, f32[12,128]{1,0:T(8,128)S(1)} %bitcast.244, f32[12,128]{1,0:T(8,128)S(1)} %bitcast.245, ...), kind=kLoop, calls=%fused_computation.80 | loop fusion | flops 10813428 | bytes 995376 | tf_op jit(solution)/shard_map/reduce_sum | solution.py:54
  179.7 2.7 %fusion.13 = bf16[12,128,128]{2,1,0:T(8,128)(2,1)} fusion(bf16[12,128,384]{2,1,0:T(8,128)(2,1)S(1)} %copy-done.3, pred[12]{0:T(512)(128)(4,1)} %copy-done.25, bf16[384,128]{1,0:T(8,128)(2,1)} %param.27, f32[12,128,128]{2,1,0:T(8,128)} %all-reduce.3.cloned.1.call-done, f32[12,128]{1,0:T(8,128)} %bitcast.265, f32[12,128]{1,0:T(8,128)S(1)} %bitcast.239, ...), kind=kOutput, calls=%fused_computation.48 | convolution fusion | flops 204079104 | bytes 2482188 | tf_op jit(solution)/shard_map/pab,pbc->pac/dot_general | solution.py:46
  182.4 4.2 %all-to-all-done.2 = bf16[4,4,128,128]{3,1,2,0:T(4,128)(2,1)S(1)} async-done(((bf16[4,4,128,128]{3,1,2,0:T(4,128)(2,1)}), bf16[4,4,128,128]{3,1,2,0:T(4,128)(2,1)S(1)}, u32[]{:S(2)}, u32[]{:S(2)}) %all-to-all-start.2) | async-done | bytes 524320 | tf_op jit(solution)/shard_map/all_to_all | solution.py:155
  187.8 27.6 %all-reduce.4 = bf16[2048,128]{1,0:T(8,128)(2,1)S(1)} all-reduce(f32[2048,128]{1,0:T(8,128)S(1)} %bitcast.224), channel_id=1, replica_groups=mesh['groups'=2,'res'=4,'blk'=2,'ch'=2] {'blk'}, use_global_device_ids=true, to_apply=%region_7.10 | all-reduce | flops 262144 | bytes 1572864 | tf_op jit(solution)/shard_map/psum | solution.py:171
  (224 shorter events, 81.2 us)
Async XLA Ops:
  7.2 208.3 %copy-start = (bf16[128,384]{1,0:T(8,128)(2,1)S(1)}, bf16[128,384]{1,0:T(8,128)(2,1)}, u32[]{:S(2)}) copy-start(bf16[128,384]{1,0:T(8,128)(2,1)} %param.31) | copy-start | bytes 294916
  12.7 7.8 %copy-start.1 = (bf16[2048,384]{1,0:T(8,128)(2,1)S(1)}, bf16[2048,384]{1,0:T(8,128)(2,1)}, u32[]{:S(2)}) copy-start(bf16[2048,384]{1,0:T(8,128)(2,1)} %param.19) | copy-start | bytes 4718596
  12.7 43.4 %all-to-all-start = ((bf16[4,4,128,384]{3,2,1,0:T(8,128)(2,1)}), bf16[4,4,128,384]{3,2,1,0:T(8,128)(2,1)S(1)}, u32[]{:S(2)}, u32[]{:S(2)}) async-start(bf16[4,4,128,384]{3,2,1,0:T(8,128)(2,1)} %broadcast_select_fusion), calls=%async_computation | async-start | bytes 3145728 | tf_op jit(solution)/shard_map/all_to_all | solution.py:119
  19.8 5.2 %copy-start.22 = (s32[12,2]{0,1:T(2,128)}, s32[12,2]{0,1:T(2,128)S(1)}, u32[]{:S(2)}) copy-start(s32[12,2]{0,1:T(2,128)S(1)} %dynamic-slice_bitcast_fusion) | copy-start | bytes 292
  19.9 5.9 %copy-start.26 = (pred[12]{0:T(512)(128)(4,1)}, pred[12]{0:T(512)(128)(4,1)S(1)}, u32[]{:S(2)}) copy-start(pred[12]{0:T(512)(128)(4,1)S(1)} %get-tuple-element.81) | copy-start | bytes 40
  25.8 35.4 %copy-start.25 = (pred[12]{0:T(512)(128)(4,1)}, pred[12]{0:T(512)(128)(4,1)S(1)}, u32[]{:S(2)}) copy-start(pred[12]{0:T(512)(128)(4,1)S(1)} %get-tuple-element.79) | copy-start | bytes 40
  25.8 33.6 %copy-start.18 = (s32[1024]{0:T(1024)}, s32[1024]{0:T(1024)S(1)}, u32[]{:S(2)}) copy-start(s32[1024]{0:T(1024)S(1)} %pad_clamp_fusion) | copy-start | bytes 12292
  56.1 90.5 %all-to-all-start.1 = ((bf16[4,4,26,128]{3,1,2,0:T(4,128)(2,1)}), bf16[4,4,26,128]{3,1,2,0:T(4,128)(2,1)S(1)}, u32[]{:S(2)}, u32[]{:S(2)}) async-start(bf16[4,4,26,128]{3,1,2,0:T(4,128)(2,1)} %fusion.42), calls=%async_computation.1 | async-start | bytes 212992 | tf_op jit(solution)/shard_map/all_to_all | solution.py:134
  59.4 104.0 %all-reduce.3.cloned.1.call-start = ((), (), s32[]{:S(2)}) async-start(), calls=%async_computation.3 | async-start | bytes 1572864 | tf_op jit(solution)/shard_map/psum | solution.py:146
  63.1 79.5 %copy-start.15 = (s32[4,4]{1,0:T(4,128)S(1)}, s32[4,4]{1,0:T(4,128)}, u32[]{:S(2)}) copy-start(s32[4,4]{1,0:T(4,128)} %get-tuple-element.63) | copy-start | bytes 196
  63.1 80.2 %copy-start.12 = (f32[12,1,128]{2,1,0:T(1,128)S(1)}, f32[12,1,128]{2,1,0:T(1,128)}, u32[]{:S(2)}) copy-start(f32[12,1,128]{2,1,0:T(1,128)} %get-tuple-element.97) | copy-start | bytes 18436
  63.1 80.3 %copy-start.11 = (f32[12,1,128]{2,1,0:T(1,128)S(1)}, f32[12,1,128]{2,1,0:T(1,128)}, u32[]{:S(2)}) copy-start(f32[12,1,128]{2,1,0:T(1,128)} %get-tuple-element.111) | copy-start | bytes 18436
  63.1 80.3 %copy-start.10 = (f32[12,1,128]{2,1,0:T(1,128)S(1)}, f32[12,1,128]{2,1,0:T(1,128)}, u32[]{:S(2)}) copy-start(f32[12,1,128]{2,1,0:T(1,128)} %get-tuple-element.112) | copy-start | bytes 18436
  63.1 83.4 %copy-start.23 = (s32[12,2]{0,1:T(2,128)S(1)}, s32[12,2]{0,1:T(2,128)}, u32[]{:S(2)}) copy-start(s32[12,2]{0,1:T(2,128)} %copy-done.22) | copy-start | bytes 292
  63.1 83.4 %copy-start.29 = (s32[12]{0:T(128)S(1)}, s32[12]{0:T(128)}, u32[]{:S(2)}) copy-start(s32[12]{0:T(128)} %copy-done.28) | copy-start | bytes 148
  142.6 20.8 %copy-start.2 = (bf16[12,128,384]{2,1,0:T(8,128)(2,1)S(1)}, bf16[12,128,384]{2,1,0:T(8,128)(2,1)}, u32[]{:S(2)}) copy-start(bf16[12,128,384]{2,1,0:T(8,128)(2,1)} %gather_fusion.2) | copy-start | bytes 3538948
  151.6 13.8 %copy-start.8 = (f32[12,1,128]{2,0,1:T(8,128)}, f32[12,1,128]{2,0,1:T(8,128)S(1)}, u32[]{:S(2)}) copy-start(f32[12,1,128]{2,0,1:T(8,128)S(1)} %copy.163) | copy-start | bytes 18436
  151.7 13.8 %copy-start.9 = (f32[12,1,128]{2,0,1:T(8,128)}, f32[12,1,128]{2,0,1:T(8,128)S(1)}, u32[]{:S(2)}) copy-start(f32[12,1,128]{2,0,1:T(8,128)S(1)} %copy.165) | copy-start | bytes 18436
  165.8 13.9 %copy-start.3 = (bf16[12,128,384]{2,1,0:T(8,128)(2,1)S(1)}, bf16[12,128,384]{2,1,0:T(8,128)(2,1)}, u32[]{:S(2)}) copy-start(bf16[12,128,384]{2,1,0:T(8,128)(2,1)} %gather_fusion.3) | copy-start | bytes 3538948
  166.8 19.8 %all-to-all-start.2 = ((bf16[4,4,128,128]{3,1,2,0:T(4,128)(2,1)}), bf16[4,4,128,128]{3,1,2,0:T(4,128)(2,1)S(1)}, u32[]{:S(2)}, u32[]{:S(2)}) async-start(bf16[4,4,128,128]{3,1,2,0:T(4,128)(2,1)} %copy.48), calls=%async_computation.2 | async-start | bytes 1048576 | tf_op jit(solution)/shard_map/all_to_all | solution.py:155
  179.7 7.1 %copy-start.24 = (s32[16]{0:T(128)S(1)}, s32[16]{0:T(128)}, u32[]{:S(2)}) copy-start(s32[16]{0:T(128)} %eq.90) | copy-start | bytes 196
  179.7 7.1 %copy-start.27 = (pred[16]{0:T(512)(128)(4,1)S(1)}, pred[16]{0:T(512)(128)(4,1)}, u32[]{:S(2)}) copy-start(pred[16]{0:T(512)(128)(4,1)} %gt.12) | copy-start | bytes 52
  182.4 4.7 %copy-start.4 = (bf16[12,128,128]{2,1,0:T(8,128)(2,1)S(1)}, bf16[12,128,128]{2,1,0:T(8,128)(2,1)}, u32[]{:S(2)}) copy-start(bf16[12,128,128]{2,1,0:T(8,128)(2,1)} %fusion.13) | copy-start | bytes 1179652
  182.4 4.7 %copy-start.21 = (s32[12]{0:T(128)S(1)}, s32[12]{0:T(128)}, u32[]{:S(2)}) copy-start(s32[12]{0:T(128)} %copy-done.20) | copy-start | bytes 148
  (10 other events, 19.6 us)
Sparse Core Ops, SparseCore 0:
  142.7 20.5 all-reduce.2
where the time goes:
time: 225 us; the launch traced here: 224 us
  matrix products  72.7 us (32%)
  waiting for transfers between devices  39.6 us (18%)
  local copies, waits for them, and re-layouts  31 us (14%)
  blocking collectives  27.6 us (12%)
  other arithmetic  23.4 us (10%)
  starting transfers between devices  14.7 us (7%)
  between operations  14.7 us (7%)
    dot_general x12, matrix products, tile_logit(): jnp.einsum('c,acb->ab', gate_vec, jnp.maximum(pair_act, 0.0), precision=l...  30.6 us
    dot_general x12, matrix products, tile_logit(): jnp.einsum('kc,akb->acb', w_pair, outer_prod, preferred_element_type=jnp....  30.3 us
    psum x1, blocking collectives, shards(): summed_rows = lax.psum(delta_rows, 'blk')  27.6 us
    all_to_all x1, waiting for transfers between devices, shards(): lax.all_to_all(row_send, 'res', split_axis=0, concat_axis=0, tiled=True)  23.7 us
    psum x1, waiting for transfers between devices, shards(): logits = lax.psum(partial_logits, 'ch')  11.7 us
    convert_element_type x12, other arithmetic, tile_logit(): near_left.astype(jnp.float32)[:, :, None]  9.25 us
    dynamic_update_slice x12, local copies, waits for them, and re-layouts, shards(): lax.scan(tile_step, jnp.zeros((), jnp.float32), (left_feats, right_feats))  7.54 us
    reduce_sum x1, other arithmetic, finish(): fape_value = jnp.sum(weight * clipped, axis=(1, 2)) / (BLOCK * BLOCK)  7.52 us
  transfers between devices with their start and end apart: 4, of which 3 were waited for; matrix products, arithmetic and copies ran while one was open for 51% of the time, Pallas kernels for 0%

commit v1 on v0

--- a/solution.py
+++ b/solution.py
@@ -143,7 +143,8 @@
     state_out, partial_logits = lax.scan(
         tile_step, jnp.zeros((), jnp.float32), (left_feats, right_feats)
     )
-    logits = lax.psum(partial_logits, "ch")
+    parts = lax.all_gather(partial_logits, "ch")
+    logits = jnp.sum(parts, axis=0)
     pair_fape, to_first, to_second = finish(logits, value_near, value_far, near_geo, far_geo)
     back_hot = (
         recv_slot[:, None] == jnp.arange(res_count * capacity, dtype=jnp.int32)[None, :]

time: 225 us -> 217 us (0.964)
  local copies, waits for them, and re-layouts: 31 us -> 21.4 us
    psum x1 -> x0, waiting for transfers between devices: 11.7 us -> none  [shards(): logits = lax.psum(partial_logits, 'ch')]
    all_gather x0 -> x1, waiting for transfers between devices: none -> 9.9 us  [shards(): parts = lax.all_gather(partial_logits, 'ch')]
    unnamed x96 -> x60, local copies, waits for them, and re-layouts: 7.31 us -> 0.2 us
  transfers between devices with their start and end apart: 4 -> 4, of which waited for: 3 -> 3; matrix products, arithmetic and copies ran while one was open for 51% -> 48% of each run, Pallas kernels for 0% -> 0%
where the time goes in v1:
time: 217 us; the launch traced here: 216 us
  matrix products  72.2 us (33%)
  waiting for transfers between devices  41.6 us (19%)
  blocking collectives  27.7 us (13%)
  other arithmetic  23.3 us (11%)
  local copies, waits for them, and re-layouts  21.4 us (10%)
  starting transfers between devices  14.7 us (7%)
  between operations  14.7 us (7%)
    dot_general x12, matrix products, tile_logit(): jnp.einsum('c,acb->ab', gate_vec, jnp.maximum(pair_act, 0.0), precision=l...  30.6 us
    dot_general x12, matrix products, tile_logit(): jnp.einsum('kc,akb->acb', w_pair, outer_prod, preferred_element_type=jnp....  30.3 us
    psum x1, blocking collectives, shards(): summed_rows = lax.psum(delta_rows, 'blk')  27.7 us
    all_to_all x1, waiting for transfers between devices, shards(): lax.all_to_all(row_send, 'res', split_axis=0, concat_axis=0, tiled=True)  25.5 us
    all_gather x1, waiting for transfers between devices, shards(): parts = lax.all_gather(partial_logits, 'ch')  9.9 us
    convert_element_type x12, other arithmetic, tile_logit(): near_left.astype(jnp.float32)[:, :, None]  9.25 us
    dynamic_update_slice x12, local copies, waits for them, and re-layouts, shards(): lax.scan(tile_step, jnp.zeros((), jnp.float32), (left_feats, right_feats))  7.53 us
    all_to_all x1, starting transfers between devices, shards(): lax.all_to_all(row_send, 'res', split_axis=0, concat_axis=0, tiled=True)  6.45 us
  transfers between devices with their start and end apart: 4, of which 3 were waited for; matrix products, arithmetic and copies ran while one was open for 48% of the time, Pallas kernels for 0%

profile of v1, /device:TPU:0, one launch (start us, length us, event | category | flops | bytes accessed | tf_op | source)
XLA Modules:
  0.0 215.8 jit_solution(16010191906731456781)
XLA Ops:
  12.2 6.4 %all-to-all-start = ((bf16[4,4,128,384]{3,2,1,0:T(8,128)(2,1)}), bf16[4,4,128,384]{3,2,1,0:T(8,128)(2,1)S(1)}, u32[]{:S(2)}, u32[]{:S(2)}) async-start(bf16[4,4,128,384]{3,2,1,0:T(8,128)(2,1)} %broadcast_select_fusion), calls=%async_computation | async-start | bytes 3145728 | tf_op jit(solution)/shard_map/all_to_all | solution.py:119
  27.5 2.5 %convolution_convert_fusion.4 = bf16[12,128,128]{2,1,0:T(8,128)(2,1)} fusion(bf16[12,128,384]{2,1,0:T(8,128)(2,1)} %gather_fusion.2, pred[12]{0:T(512)(128)(4,1)S(1)} %get-tuple-element.81, bf16[384,128]{1,0:T(8,128)(2,1)} %param.25), kind=kOutput, calls=%fused_computation.52 | convolution fusion | flops 151781376 | bytes 1671180 | tf_op jit(solution)/shard_map/pad,dc->pac/dot_general | solution.py:122
  30.0 25.5 %all-to-all-done = bf16[4,4,128,384]{3,2,1,0:T(8,128)(2,1)S(1)} async-done(((bf16[4,4,128,384]{3,2,1,0:T(8,128)(2,1)}), bf16[4,4,128,384]{3,2,1,0:T(8,128)(2,1)S(1)}, u32[]{:S(2)}, u32[]{:S(2)}) %all-to-all-start) | async-done | bytes 1572896 | tf_op jit(solution)/shard_map/all_to_all | solution.py:119
  55.6 3.3 %all-to-all-start.1 = ((bf16[4,4,26,128]{3,1,2,0:T(4,128)(2,1)}), bf16[4,4,26,128]{3,1,2,0:T(4,128)(2,1)S(1)}, u32[]{:S(2)}, u32[]{:S(2)}) async-start(bf16[4,4,26,128]{3,1,2,0:T(4,128)(2,1)} %fusion.42), calls=%async_computation.1 | async-start | bytes 212992 | tf_op jit(solution)/shard_map/all_to_all | solution.py:134
  62.6 79.4 %while.11 = (s32[]{:T(128)}, f32[12,128,128]{2,1,0:T(8,128)}, bf16[12,128,128]{2,1,0:T(8,128)(2,1)}, bf16[12,128,128]{2,1,0:T(8,128)(2,1)S(1)}, bf16[128,64]{0,1...) while((s32[]{:T(128)}, f32[12,128,128]{2,1,0:T(8,128)}, bf16[12,128,128]{2,1,0:T(8,128)(2,1)}, ...), condition=%wide.region_5.7_spmd.clone, body=%wide.region_4.6_spmd.sunk.clone | while | flops 287342592 | bytes 9061461 | solution.py:143
  63.5 2.5 %fusion.98 = f32[128,128,64]{1,2,0:T(8,128)S(1)} fusion(f32[128,128]{1,0:T(8,128)S(1)} %convert_bitcast_fusion.3, f32[128,128]{1,0:T(8,128)S(1)} %bitcast_convert_fusion.3, bf16[128,64]{0,1:T(8,128)(2,1)S(1)} %get-tuple-element.198), kind=kOutput, calls=%fused_computation.7.clone.1.clone | convolution fusion | flops 272629760 | bytes 4341760 | tf_op jit(solution)/shard_map/while/body/eval_jaxpr/kc,akb->acb/dot_general | solution.py:13
  66.1 2.5 %fusion.99 = f32[1,128,128]{2,0,1:T(1,128)S(1)} fusion(f32[128,128,64]{1,2,0:T(8,128)S(1)} %fusion.98, f32[64]{0:T(128)S(1)} %get-tuple-element.199, f32[64]{0:T(128)S(1)} %get-tuple-element.200), kind=kOutput, calls=%fused_computation.8.clone.1.clone | convolution fusion | flops 14680064 | bytes 4260352 | tf_op jit(solution)/shard_map/while/body/eval_jaxpr/c,acb->ab/dot_general | solution.py:15
  72.7 2.5 %fusion.99 = f32[1,128,128]{2,0,1:T(1,128)S(1)} fusion(f32[128,128,64]{1,2,0:T(8,128)S(1)} %fusion.98, f32[64]{0:T(128)S(1)} %get-tuple-element.199, f32[64]{0:T(128)S(1)} %get-tuple-element.200), kind=kOutput, calls=%fused_computation.8.clone.1.clone | convolution fusion | flops 14680064 | bytes 4260352 | tf_op jit(solution)/shard_map/while/body/eval_jaxpr/c,acb->ab/dot_general | solution.py:15
  79.3 2.5 %fusion.99 = f32[1,128,128]{2,0,1:T(1,128)S(1)} fusion(f32[128,128,64]{1,2,0:T(8,128)S(1)} %fusion.98, f32[64]{0:T(128)S(1)} %get-tuple-element.199, f32[64]{0:T(128)S(1)} %get-tuple-element.200), kind=kOutput, calls=%fused_computation.8.clone.1.clone | convolution fusion | flops 14680064 | bytes 4260352 | tf_op jit(solution)/shard_map/while/body/eval_jaxpr/c,acb->ab/dot_general | solution.py:15
  85.9 2.5 %fusion.99 = f32[1,128,128]{2,0,1:T(1,128)S(1)} fusion(f32[128,128,64]{1,2,0:T(8,128)S(1)} %fusion.98, f32[64]{0:T(128)S(1)} %get-tuple-element.199, f32[64]{0:T(128)S(1)} %get-tuple-element.200), kind=kOutput, calls=%fused_computation.8.clone.1.clone | convolution fusion | flops 14680064 | bytes 4260352 | tf_op jit(solution)/shard_map/while/body/eval_jaxpr/c,acb->ab/dot_general | solution.py:15
  92.5 2.5 %fusion.99 = f32[1,128,128]{2,0,1:T(1,128)S(1)} fusion(f32[128,128,64]{1,2,0:T(8,128)S(1)} %fusion.98, f32[64]{0:T(128)S(1)} %get-tuple-element.199, f32[64]{0:T(128)S(1)} %get-tuple-element.200), kind=kOutput, calls=%fused_computation.8.clone.1.clone | convolution fusion | flops 14680064 | bytes 4260352 | tf_op jit(solution)/shard_map/while/body/eval_jaxpr/c,acb->ab/dot_general | solution.py:15
  99.1 2.5 %fusion.99 = f32[1,128,128]{2,0,1:T(1,128)S(1)} fusion(f32[128,128,64]{1,2,0:T(8,128)S(1)} %fusion.98, f32[64]{0:T(128)S(1)} %get-tuple-element.199, f32[64]{0:T(128)S(1)} %get-tuple-element.200), kind=kOutput, calls=%fused_computation.8.clone.1.clone | convolution fusion | flops 14680064 | bytes 4260352 | tf_op jit(solution)/shard_map/while/body/eval_jaxpr/c,acb->ab/dot_general | solution.py:15
  105.8 2.5 %fusion.99 = f32[1,128,128]{2,0,1:T(1,128)S(1)} fusion(f32[128,128,64]{1,2,0:T(8,128)S(1)} %fusion.98, f32[64]{0:T(128)S(1)} %get-tuple-element.199, f32[64]{0:T(128)S(1)} %get-tuple-element.200), kind=kOutput, calls=%fused_computation.8.clone.1.clone | convolution fusion | flops 14680064 | bytes 4260352 | tf_op jit(solution)/shard_map/while/body/eval_jaxpr/c,acb->ab/dot_general | solution.py:15
  112.4 2.5 %fusion.99 = f32[1,128,128]{2,0,1:T(1,128)S(1)} fusion(f32[128,128,64]{1,2,0:T(8,128)S(1)} %fusion.98, f32[64]{0:T(128)S(1)} %get-tuple-element.199, f32[64]{0:T(128)S(1)} %get-tuple-element.200), kind=kOutput, calls=%fused_computation.8.clone.1.clone | convolution fusion | flops 14680064 | bytes 4260352 | tf_op jit(solution)/shard_map/while/body/eval_jaxpr/c,acb->ab/dot_general | solution.py:15
  119.0 2.5 %fusion.99 = f32[1,128,128]{2,0,1:T(1,128)S(1)} fusion(f32[128,128,64]{1,2,0:T(8,128)S(1)} %fusion.98, f32[64]{0:T(128)S(1)} %get-tuple-element.199, f32[64]{0:T(128)S(1)} %get-tuple-element.200), kind=kOutput, calls=%fused_computation.8.clone.1.clone | convolution fusion | flops 14680064 | bytes 4260352 | tf_op jit(solution)/shard_map/while/body/eval_jaxpr/c,acb->ab/dot_general | solution.py:15
  125.6 2.5 %fusion.99 = f32[1,128,128]{2,0,1:T(1,128)S(1)} fusion(f32[128,128,64]{1,2,0:T(8,128)S(1)} %fusion.98, f32[64]{0:T(128)S(1)} %get-tuple-element.199, f32[64]{0:T(128)S(1)} %get-tuple-element.200), kind=kOutput, calls=%fused_computation.8.clone.1.clone | convolution fusion | flops 14680064 | bytes 4260352 | tf_op jit(solution)/shard_map/while/body/eval_jaxpr/c,acb->ab/dot_general | solution.py:15
  129.7 2.5 %fusion.98 = f32[128,128,64]{1,2,0:T(8,128)S(1)} fusion(f32[128,128]{1,0:T(8,128)S(1)} %convert_bitcast_fusion.3, f32[128,128]{1,0:T(8,128)S(1)} %bitcast_convert_fusion.3, bf16[128,64]{0,1:T(8,128)(2,1)S(1)} %get-tuple-element.198), kind=kOutput, calls=%fused_computation.7.clone.1.clone | convolution fusion | flops 272629760 | bytes 4341760 | tf_op jit(solution)/shard_map/while/body/eval_jaxpr/kc,akb->acb/dot_general | solution.py:13
  132.2 2.6 %fusion.99 = f32[1,128,128]{2,0,1:T(1,128)S(1)} fusion(f32[128,128,64]{1,2,0:T(8,128)S(1)} %fusion.98, f32[64]{0:T(128)S(1)} %get-tuple-element.199, f32[64]{0:T(128)S(1)} %get-tuple-element.200), kind=kOutput, calls=%fused_computation.8.clone.1.clone | convolution fusion | flops 14680064 | bytes 4260352 | tf_op jit(solution)/shard_map/while/body/eval_jaxpr/c,acb->ab/dot_general | solution.py:15
  138.9 2.5 %fusion.99 = f32[1,128,128]{2,0,1:T(1,128)S(1)} fusion(f32[128,128,64]{1,2,0:T(8,128)S(1)} %fusion.98, f32[64]{0:T(128)S(1)} %get-tuple-element.199, f32[64]{0:T(128)S(1)} %get-tuple-element.200), kind=kOutput, calls=%fused_computation.8.clone.1.clone | convolution fusion | flops 14680064 | bytes 4260352 | tf_op jit(solution)/shard_map/while/body/eval_jaxpr/c,acb->ab/dot_general | solution.py:15
  143.5 9.9 %all-gather.3.cloned.1.call-done = f32[24,128,128]{2,1,0:T(8,128)} async-done(((f32[12,128,128]{2,1,0:T(8,128)}), f32[24,128,128]{2,1,0:T(8,128)}) %all-gather.3.cloned.1.call-update) | async-done | bytes 1572880 | tf_op jit(solution)/shard_map/all_gather | solution.py:146
  158.5 4.9 %all-to-all-start.2 = ((bf16[4,4,128,128]{3,1,2,0:T(4,128)(2,1)}), bf16[4,4,128,128]{3,1,2,0:T(4,128)(2,1)S(1)}, u32[]{:S(2)}, u32[]{:S(2)}) async-start(bf16[4,4,128,128]{3,1,2,0:T(4,128)(2,1)} %copy.48), calls=%async_computation.2 | async-start | bytes 1048576 | tf_op jit(solution)/shard_map/all_to_all | solution.py:156
  163.4 6.3 %fusion.38 = f32[12]{0:T(128)S(1)} fusion(f32[12,128]{1,0:T(8,128)S(1)} %bitcast.235, f32[12,128]{1,0:T(8,128)S(1)} %bitcast.236, f32[12,128]{1,0:T(8,128)S(1)} %bitcast.237, f32[12,128]{1,0:T(8,128)S(1)} %bitcast.238, f32[12,128]{1,0:T(8,128)S(1)} %bitcast.239, f32[12,128]{1,0:T(8,128)S(1)} %bitcast.240, f32[12,128]{1,0:T(8,128)S(1)} %bitcast.241, ...), kind=kLoop, calls=%fused_computation.80 | loop fusion | flops 10813428 | bytes 995376 | tf_op jit(solution)/shard_map/reduce_sum | solution.py:54
  172.3 6.1 %all-to-all-done.2 = bf16[4,4,128,128]{3,1,2,0:T(4,128)(2,1)S(1)} async-done(((bf16[4,4,128,128]{3,1,2,0:T(4,128)(2,1)}), bf16[4,4,128,128]{3,1,2,0:T(4,128)(2,1)S(1)}, u32[]{:S(2)}, u32[]{:S(2)}) %all-to-all-start.2) | async-done | bytes 524320 | tf_op jit(solution)/shard_map/all_to_all | solution.py:156
  179.5 27.7 %all-reduce.1 = bf16[2048,128]{1,0:T(8,128)(2,1)S(1)} all-reduce(f32[2048,128]{1,0:T(8,128)S(1)} %bitcast.225), channel_id=1, replica_groups=mesh['groups'=2,'res'=4,'blk'=2,'ch'=2] {'blk'}, use_global_device_ids=true, to_apply=%region_7.10 | all-reduce | flops 262144 | bytes 1572864 | tf_op jit(solution)/shard_map/psum | solution.py:172
  (189 shorter events, 72.5 us)
Async XLA Ops:
  7.2 200.1 %copy-start = (bf16[128,384]{1,0:T(8,128)(2,1)S(1)}, bf16[128,384]{1,0:T(8,128)(2,1)}, u32[]{:S(2)}) copy-start(bf16[128,384]{1,0:T(8,128)(2,1)} %param.31) | copy-start | bytes 294916
  12.2 7.7 %copy-start.1 = (bf16[2048,384]{1,0:T(8,128)(2,1)S(1)}, bf16[2048,384]{1,0:T(8,128)(2,1)}, u32[]{:S(2)}) copy-start(bf16[2048,384]{1,0:T(8,128)(2,1)} %param.19) | copy-start | bytes 4718596
  12.2 43.4 %all-to-all-start = ((bf16[4,4,128,384]{3,2,1,0:T(8,128)(2,1)}), bf16[4,4,128,384]{3,2,1,0:T(8,128)(2,1)S(1)}, u32[]{:S(2)}, u32[]{:S(2)}) async-start(bf16[4,4,128,384]{3,2,1,0:T(8,128)(2,1)} %broadcast_select_fusion), calls=%async_computation | async-start | bytes 3145728 | tf_op jit(solution)/shard_map/all_to_all | solution.py:119
  18.6 3.1 %copy-start.4 = (f32[12,2048]{1,0:T(8,128)S(1)}, f32[12,2048]{1,0:T(8,128)}, u32[]{:S(2)}) copy-start(f32[12,2048]{1,0:T(8,128)} %param.20) | copy-start | bytes 294916
  18.6 3.1 %copy-start.5 = (f32[12,2048]{1,0:T(8,128)S(1)}, f32[12,2048]{1,0:T(8,128)}, u32[]{:S(2)}) copy-start(f32[12,2048]{1,0:T(8,128)} %param.21) | copy-start | bytes 294916
  19.9 2.0 copy-start.8
  19.9 2.0 copy-start.9
  30.0 30.7 %copy-start.10 = (bf16[384,128]{1,0:T(8,128)(2,1)S(1)}, bf16[384,128]{1,0:T(8,128)(2,1)}, u32[]{:S(2)}) copy-start(bf16[384,128]{1,0:T(8,128)(2,1)} %param.26) | copy-start | bytes 294916
  55.6 87.1 %all-to-all-start.1 = ((bf16[4,4,26,128]{3,1,2,0:T(4,128)(2,1)}), bf16[4,4,26,128]{3,1,2,0:T(4,128)(2,1)S(1)}, u32[]{:S(2)}, u32[]{:S(2)}) async-start(bf16[4,4,26,128]{3,1,2,0:T(4,128)(2,1)} %fusion.42), calls=%async_computation.1 | async-start | bytes 212992 | tf_op jit(solution)/shard_map/all_to_all | solution.py:134
  58.9 94.5 %all-gather.3.cloned.1.call-start = ((), (), s32[]{:S(2)}) async-start(), calls=%async_computation.3 | async-start | bytes 2359296 | tf_op jit(solution)/shard_map/all_gather | solution.py:146
  60.7 1.9 copy-start.3
  60.7 1.9 copy-start.6
  60.7 1.9 copy-start.7
  62.6 79.5 %copy-start.2 = (f32[12,26,128]{2,1,0:T(8,128)S(1)}, f32[12,26,128]{2,1,0:T(8,128)}, u32[]{:S(2)}) copy-start(f32[12,26,128]{2,1,0:T(8,128)} %gather_fusion.4) | copy-start | bytes 479236
  143.3 11.7 %copy-start.11 = (bf16[384,128]{1,0:T(8,128)(2,1)S(1)}, bf16[384,128]{1,0:T(8,128)(2,1)}, u32[]{:S(2)}) copy-start(bf16[384,128]{1,0:T(8,128)(2,1)} %param.27) | copy-start | bytes 294916
  158.5 19.8 %all-to-all-start.2 = ((bf16[4,4,128,128]{3,1,2,0:T(4,128)(2,1)}), bf16[4,4,128,128]{3,1,2,0:T(4,128)(2,1)S(1)}, u32[]{:S(2)}, u32[]{:S(2)}) async-start(bf16[4,4,128,128]{3,1,2,0:T(4,128)(2,1)} %copy.48), calls=%async_computation.2 | async-start | bytes 1048576 | tf_op jit(solution)/shard_map/all_to_all | solution.py:156
Sparse Core Ops, SparseCore 0:
  142.2 11.1 all-gather.2
